TPU v7x, 128 devices: a whole 4x4x4 slice. The times are simulated.
128 devices in a mesh: gx: 16 (over y, x_hi, core), gy: 8 (over x_lo, z).
Axes of the slice: x: 4 (x_hi: 2, x_lo: 2; x = x_hi * 2 + x_lo), y: 4, z: 4, core: 2. Of those that a mesh axis runs over, the one named last changes fastest.
Arguments:
- tracer: float32 [2, 16, 3584, 2048], P(None, None, 'gx', 'gy'), may hold values from -6 to 6
- zonal_flow: bfloat16 [16, 3584, 2048], P(None, 'gx', 'gy'), may hold values from -3 to 3
- meridional_flow: bfloat16 [16, 3584, 2048], P(None, 'gx', 'gy'), may hold values from -3 to 3
- surface_prev: float32 [3584, 2048], P('gx', 'gy'), may hold values from -6 to 6
- transport_x: float32 [3584, 2048], P('gx', 'gy'), may hold values from -6 to 6
- transport_y: float32 [3584, 2048], P('gx', 'gy'), may hold values from -6 to 6
- land_mask: int32 [3584, 2048], P('gx', 'gy'), may hold values 0 or 1
- levels: int32 [3584, 2048], P('gx', 'gy'), may hold values from 1 to 16
Outputs:
- tracer_next: float32 [2, 16, 3584, 2048], P(None, None, 'gx', 'gy')
- surface: float32 [3584, 2048], P('gx', 'gy')
- transport_x_next: float32 [3584, 2048], P('gx', 'gy')
- transport_y_next: float32 [3584, 2048], P('gx', 'gy')
All inputs are finite; a program needn't handle non-finite values. No bound on the sum of `land_mask` on one device may be relied on, other than what follows from the above.
Results may differ from a plain program's by a relative error of at most 0.0003.
Values sent between devices are 32-bit elements; how exact they have to be, the bound alone decides.
A program may use at most 192 MiB of HBM per device.

v0:
```python
import jax
import jax.numpy as jnp
from jax import lax
from jax.experimental import pallas as pl
from jax.experimental.pallas import tpu as pltpu
from jax.sharding import PartitionSpec as P

MESH = pl.DeviceIdType.MESH
F32 = jnp.float32
I32 = jnp.int32

LEVELS = 16
ROWS = 224
COLS = 256
LANES = 128
HALO = 8
FIRST = 16
LAST = FIRST + ROWS
EXT = 256
GROUP = 32
NGROUPS = ROWS // GROUP
CHUNK = 16
NCHUNKS = ROWS // CHUNK
EARLY_GROUPS = 2
FIRST_CHUNKS = 2
STEP_CHUNKS = 11


def lane_ids(rows):
    return lax.broadcasted_iota(I32, (rows, LANES), 1)


def to_north(tiles, lanes):
    moved = [pltpu.roll(t, LANES - 1, 1) for t in tiles]
    n = len(tiles)
    return [jnp.where(lanes == LANES - 1, moved[(i + 1) % n], moved[i]) for i in range(n)]


def to_south(tiles, lanes):
    moved = [pltpu.roll(t, 1, 1) for t in tiles]
    n = len(tiles)
    return [jnp.where(lanes == 0, moved[(i - 1) % n], moved[i]) for i in range(n)]


def nine_sum(ref, r0, rows, lanes):
    sides, inner = [], []
    for t in range(3):
        here = ref[t, pl.ds(r0, rows), :]
        pair = ref[t, pl.ds(r0 + 1, rows), :] + ref[t, pl.ds(r0 - 1, rows), :]
        sides.append(pair)
        inner.append(here + 0.5 * pair)
    north = to_north(inner, lanes)
    south = to_south(inner, lanes)
    return [sides[t] + (north[t] + south[t]) for t in range(3)]


def tracer_chunk(i, trs, us, vs, psc, own, cnt, edge, out, out_row):
    lanes16 = lane_ids(CHUNK)
    top, bottom = lanes16 == LANES - 1, lanes16 == 0
    r0 = pl.multiple_of(i * CHUNK, CHUNK)
    rows = pl.ds(r0, CHUNK)
    halo = r0 + HALO
    beside = edge[rows, :]
    depth = [own[2, t, rows, :] for t in range(2)]
    for k in range(LEVELS):
        half, shift = k // 8, 3 * (k % 8)
        coef = []
        for t in range(2):
            lanes = pl.ds(t * LANES, LANES)
            wet = depth[t] > float(k)
            fifth = jnp.where(wet, 0.2, 0.0)
            quarter = jnp.where(wet, 0.25, 0.0)
            fast_x = us[k, rows, lanes].astype(F32) * quarter
            fast_y = vs[k, rows, lanes].astype(F32) * quarter
            number = jnp.right_shift(cnt[half, t, rows, :], shift) & 7
            centre = 1.0 - 0.2 * number.astype(F32)
            coef.append((centre, fifth - fast_x, fifth + fast_x, fifth - fast_y, fifth + fast_y))
        for c in range(2):
            plane = c * LEVELS + k
            here = [psc[plane, t, pl.ds(halo, CHUNK), :] for t in range(2)]
            ends = pltpu.roll(beside, LANES - 1 - 2 * plane, 1)
            up = [pltpu.roll(p, LANES - 1, 1) for p in here]
            down = [pltpu.roll(p, 1, 1) for p in here]
            north_p = [jnp.where(top, up[1], up[0]), jnp.where(top, ends, up[1])]
            south_p = [jnp.where(bottom, ends, down[0]), jnp.where(bottom, down[0], down[1])]
            for t in range(2):
                lanes = pl.ds(t * LANES, LANES)
                centre, k_e, k_w, k_n, k_s = coef[t]
                value = centre * trs[c, k, rows, lanes]
                value = value + k_e * psc[plane, t, pl.ds(halo + 1, CHUNK), :]
                value = value + k_w * psc[plane, t, pl.ds(halo - 1, CHUNK), :]
                out[c, k, pl.ds(out_row, CHUNK), lanes] = value + (
                    k_n * north_p[t] + k_s * south_p[t]
                )


def step_kernel(
    tr_hbm, u_hbm, v_hbm, e0_hbm, tx_hbm, ty_hbm, mask_hbm, lev_hbm,
    out_ref, ext_ref, own_ref, peak_ref, trs, us, vs, psc, cnt, edge,
    mask_s, lev_s, raw_s,
    lx, fx, mx, a1, a2, inv, xa, ya, xb, yb, zx,
    row_e, row_w, got_e, got_w, pack, turned_p, col_n, col_s, got_n, got_s,
    l_n, l_s, l_th, l_co, f_n, f_s, f_th, f_co,
    mine, mid, max_x, max_y,
    in_sem, tr_sem, uv_sem, send_sem, recv_sem,
):
    gx = lax.axis_index("gx")
    gy = lax.axis_index("gy")
    nx, ny = 16, 8
    east, west = lax.rem(gx + 1, nx), lax.rem(gx + nx - 1, nx)
    north, south = lax.rem(gy + 1, ny), lax.rem(gy + ny - 1, ny)
    corners = ((east, north), (east, south), (west, north), (west, south))
    ring, x_hi, core = gx // 4, lax.rem(gx // 2, 2), lax.rem(gx, 2)
    plane_mates = [
        (ring * 4 + lax.rem(x_hi + d // 8, 2) * 2 + core, lax.rem(gy + d % 8, ny))
        for d in range(1, 16)
    ]
    line_mates = [
        (lax.rem(ring + d % 4, 4) * 4 + x_hi * 2 + lax.rem(core + d // 4, 2), gy)
        for d in range(1, 8)
    ]
    sides = ((east, gy), (west, gy), (gx, north), (gx, south))

    barrier = pltpu.get_barrier_semaphore()
    greeted = (*plane_mates, *line_mates, *sides, *corners)
    for mate in greeted:
        pl.semaphore_signal(barrier, inc=1, device_id=mate, device_id_type=MESH)

    def flat_copy(src, dst, slot):
        copies = []
        for t in range(2):
            copies.append(
                pltpu.make_async_copy(
                    src.at[:, pl.ds(t * LANES, LANES)], dst(t), in_sem.at[2 * slot + t]
                )
            )
        for c in copies:
            c.start()
        return copies

    c_mask = flat_copy(mask_hbm, lambda t: mask_s.at[t], 0)
    c_lev = flat_copy(lev_hbm, lambda t: lev_s.at[t], 1)
    c_tx = flat_copy(tx_hbm, lambda t: raw_s.at[0, t], 2)
    c_ty = flat_copy(ty_hbm, lambda t: raw_s.at[1, t], 3)
    c_e0 = flat_copy(e0_hbm, lambda t: fx.at[0, t, pl.ds(FIRST, ROWS), :], 4)

    def group_copy(g):
        rows = pl.ds(pl.multiple_of(g * GROUP, GROUP), GROUP)
        return pltpu.make_async_copy(
            tr_hbm.at[:, :, rows, :], trs.at[:, :, rows, :], tr_sem.at[g]
        )

    for g in range(NGROUPS):
        group_copy(g).start()
    c_u = pltpu.make_async_copy(u_hbm, us, uv_sem.at[0])
    c_v = pltpu.make_async_copy(v_hbm, vs, uv_sem.at[1])

    for ref in (mx, lx, xa, ya, xb, yb):
        for t in range(3):
            ref[t, pl.ds(0, HALO), :] = jnp.zeros((HALO, LANES), F32)
            ref[t, pl.ds(EXT - HALO, HALO), :] = jnp.zeros((HALO, LANES), F32)

    pack[pl.ds(ROWS, 2 * LANES - ROWS), :] = jnp.zeros((2 * LANES - ROWS, LANES), F32)

    for c in c_mask + c_lev:
        c.wait()
    for t in range(2):
        depth = (lev_s[t] * mask_s[t]).astype(F32)
        lx[t, pl.ds(FIRST, ROWS), :] = depth
        own_ref[2, t] = depth
        mx[t, pl.ds(FIRST, ROWS), :] = jnp.where(depth > 0.0, 1.0, 0.0)
        turned = jnp.transpose(depth)
        if t == 0:
            l_s[...] = turned[:HALO]
        else:
            l_n[...] = turned[LANES - HALO :]
    for c in c_tx + c_ty + c_e0:
        c.wait()
    for t in range(2):
        wet = lx[t, pl.ds(FIRST, ROWS), :] > 0.0
        for i in range(2):
            value = jnp.where(wet, raw_s[i, t], 0.0)
            own_ref[i, t] = value
            fx[1 + i, t, pl.ds(FIRST, ROWS), :] = value

    def turn_edges(f):
        f_s[f] = jnp.transpose(fx[f, 0, pl.ds(FIRST, ROWS), :])[:HALO]
        f_n[f] = jnp.transpose(fx[f, 1, pl.ds(FIRST, ROWS), :])[LANES - HALO :]

    for f in range(3):
        turn_edges(f)

    glanes = lane_ids(GROUP)

    def force_group(g, carry):
        group_copy(g).wait()
        r0 = pl.multiple_of(g * GROUP, GROUP)
        depth = [lx[t, pl.ds(r0 + FIRST, GROUP), :] for t in range(2)]
        total = [jnp.zeros((GROUP, LANES), F32) for _ in range(2)]
        cols = jnp.zeros((GROUP, LANES), F32)
        for k in range(LEVELS):
            kept = {}
            for t in range(2):
                lanes = pl.ds(t * LANES, LANES)
                left = depth[t] - float(k)
                wet = left > 0.0
                t0 = trs[0, k, pl.ds(r0, GROUP), lanes]
                t1 = trs[1, k, pl.ds(r0, GROUP), lanes]
                total[t] = total[t] + jnp.maximum(left, 0.0) * (0.8 * t0 - 0.6 * t1)
                for i, value in enumerate((t0, t1)):
                    plane = i * LEVELS + k
                    value = jnp.where(wet, value, 0.0)
                    psc[plane, t, pl.ds(r0 + HALO, GROUP), :] = value
                    kept[t, i] = value
            for i in range(2):
                lane = 2 * (i * LEVELS + k)
                moved = pltpu.roll(jnp.where(glanes == 0, kept[0, i], kept[1, i]), lane + 1, 1)
                cols = jnp.where((glanes >= lane) & (glanes <= lane + 1), moved, cols)
        pack[pl.ds(r0, GROUP), :] = cols
        for t in range(2):
            rows = pl.ds(r0 + FIRST, GROUP)
            fx[3, t, rows, :] = total[t] * (1.0 / LEVELS) + 0.5 * fx[0, t, rows, :]
        return carry

    lax.fori_loop(0, EARLY_GROUPS, force_group, 0)
    c_u.start()
    c_v.start()

    pl.semaphore_wait(barrier, len(greeted))

    started = [0]

    def remote(src, dst, who):
        slot = started[0]
        started[0] += 1
        copy = pltpu.make_async_remote_copy(
            src_ref=src,
            dst_ref=dst,
            send_sem=send_sem.at[slot],
            recv_sem=recv_sem.at[slot],
            device_id=who,
            device_id_type=MESH,
        )
        copy.start()
        return copy

    high, low = pl.ds(LAST - HALO, HALO), pl.ds(FIRST, HALO)
    below, above = pl.ds(FIRST - HALO, HALO), pl.ds(LAST, HALO)
    both = pl.ds(0, 2)
    depth_copies = [
        remote(lx.at[1, high, :], l_co.at[0], (east, north)),
        remote(lx.at[0, high, :], l_co.at[1], (east, south)),
        remote(lx.at[1, low, :], l_co.at[2], (west, north)),
        remote(lx.at[0, low, :], l_co.at[3], (west, south)),
        remote(lx.at[both, high, :], lx.at[both, below, :], (east, gy)),
        remote(lx.at[both, low, :], lx.at[both, above, :], (west, gy)),
        remote(l_n, l_th.at[pl.ds(LANES - HALO, HALO), :], (gx, north)),
        remote(l_s, l_th.at[pl.ds(0, HALO), :], (gx, south)),
    ]

    def send_fields(which):
        return [
            remote(fx.at[which, both, high, :], fx.at[which, both, below, :], (east, gy)),
            remote(fx.at[which, both, low, :], fx.at[which, both, above, :], (west, gy)),
            remote(f_n.at[which], f_th.at[which, pl.ds(LANES - HALO, HALO), :], (gx, north)),
            remote(f_s.at[which], f_th.at[which, pl.ds(0, HALO), :], (gx, south)),
            remote(fx.at[which, 1, high, :], f_co.at[0, which], (east, north)),
            remote(fx.at[which, 0, high, :], f_co.at[1, which], (east, south)),
            remote(fx.at[which, 1, low, :], f_co.at[2, which], (west, north)),
            remote(fx.at[which, 0, low, :], f_co.at[3, which], (west, south)),
        ]

    field_copies = send_fields(pl.ds(0, 3))

    lax.fori_loop(EARLY_GROUPS, NGROUPS, force_group, 0)
    for plane in range(2 * LEVELS):
        for t in range(2):
            row_w[pl.ds(2 * plane + t, 1), :] = psc[plane, t, pl.ds(HALO, 1), :]
            row_e[pl.ds(2 * plane + t, 1), :] = psc[plane, t, pl.ds(HALO + ROWS - 1, 1), :]
    planes = 2 * LEVELS
    for h in range(2):
        turned_p[h] = jnp.transpose(pack[pl.ds(h * LANES, LANES), :])
        col_n[h] = turned_p[h, pl.ds(0, planes, stride=2), :]
        col_s[h] = turned_p[h, pl.ds(1, planes, stride=2), :]
    tracer_copies = [
        remote(row_e, got_w, (east, gy)),
        remote(row_w, got_e, (west, gy)),
        remote(col_n, got_s, (gx, north)),
        remote(col_s, got_n, (gx, south)),
    ]
    turn_edges(3)
    force_copies = send_fields(pl.ds(3, 1))

    lanes8 = lane_ids(HALO)
    lanes_all = lane_ids(ROWS)

    def inside(lanes):
        return ((lanes < HALO) & (gy < ny - 1)) | ((lanes >= LANES - HALO) & (gy > 0))

    def third_tile(dst, turned, co):
        keep8 = inside(lanes8)
        dst[2, pl.ds(FIRST, ROWS), :] = jnp.where(inside(lanes_all), jnp.transpose(turned), 0.0)
        dst[2, below, :] = jnp.where(keep8, jnp.where(lanes8 < HALO, co[1], co[0]), 0.0)
        dst[2, above, :] = jnp.where(keep8, jnp.where(lanes8 < HALO, co[3], co[2]), 0.0)

    for c in depth_copies:
        c.wait_recv()
    third_tile(lx, l_th[...], [l_co[i] for i in range(4)])

    n_tiles = (EXT - 2 * HALO) // HALO
    for i in range(n_tiles):
        rows = pl.ds(HALO + i * HALO, HALO)
        for t in range(3):
            if t == 2 or i == 0 or i == n_tiles - 1:
                mx[t, rows, :] = jnp.where(lx[t, rows, :] > 0.0, 1.0, 0.0)

    largest = jnp.zeros((HALO, LANES), F32)
    for i in range(n_tiles):
        r0 = HALO + i * HALO
        rows = pl.ds(r0, HALO)
        sum_m = nine_sum(mx, r0, HALO, lanes8)
        sum_l = nine_sum(lx, r0, HALO, lanes8)
        for t in range(3):
            value = 0.5 + 0.125 * (lx[t, rows, :] * sum_m[t] + mx[t, rows, :] * sum_l[t])
            inv[t, rows, :] = value
            if t < 2 and FIRST <= r0 < LAST:
                largest = jnp.maximum(largest, value)
    mine[...] = largest

    across = [remote(mine, max_x.at[d], mate) for d, mate in enumerate(plane_mates)]

    keep8 = inside(lanes8)
    for i in range(n_tiles):
        rows = pl.ds(HALO + i * HALO, HALO)
        for t in range(3):
            recip = 1.0 / inv[t, rows, :]
            if t == 2:
                recip = jnp.where(keep8, recip, 0.0)
            inv[t, rows, :] = recip
            eighth = 0.125 * recip
            a1[t, rows, :] = eighth * lx[t, rows, :]
            a2[t, rows, :] = eighth * mx[t, rows, :]

    for c in field_copies:
        c.wait_recv()
    for f in range(3):
        third_tile(fx.at[f], f_th[f], [f_co[i, f] for i in range(4)])
    for i in range(n_tiles):
        rows = pl.ds(HALO + i * HALO, HALO)
        for t in range(3):
            value = fx[0, t, rows, :]
            ext_ref[0, t, rows, :] = value
            xa[t, rows, :] = mx[t, rows, :] * value
            ya[t, rows, :] = lx[t, rows, :] * value

    def apply(x_ref, y_ref, r0):
        rows = pl.ds(r0, HALO)
        sum_x = nine_sum(x_ref, r0, HALO, lanes8)
        sum_y = nine_sum(y_ref, r0, HALO, lanes8)
        return [a1[t, rows, :] * sum_x[t] + a2[t, rows, :] * sum_y[t] for t in range(3)]

    for i in range(n_tiles):
        r0 = HALO + i * HALO
        rows = pl.ds(r0, HALO)
        moved = apply(xa, ya, r0)
        flux = [fx[2, t, rows, :] for t in range(3)]
        flux_n, flux_s = to_north(flux, lanes8), to_south(flux, lanes8)
        for t in range(3):
            div = fx[1, t, pl.ds(r0 + 1, HALO), :] - fx[1, t, pl.ds(r0 - 1, HALO), :]
            div = div + (flux_n[t] - flux_s[t])
            zx[t, rows, :] = (moved[t] - fx[0, t, rows, :]) - 0.25 * inv[t, rows, :] * div

    def marks(depth, base):
        count = jnp.clip(depth.astype(I32) - base, 0, 8)
        return jnp.left_shift(jnp.ones_like(count), 3 * count) - 1

    each = 0o11111111
    for i in range(ROWS // HALO):
        r0 = FIRST + i * HALO
        rows = pl.ds(r0, HALO)
        for half in range(2):
            base = 8 * half
            here = [marks(lx[t, rows, :], base) for t in range(3)]
            bits = [h & each for h in here]
            n_bits, s_bits = to_north(bits, lanes8), to_south(bits, lanes8)
            for t in range(2):
                e_bits = marks(lx[t, pl.ds(r0 + 1, HALO), :], base) & each
                w_bits = marks(lx[t, pl.ds(r0 - 1, HALO), :], base) & each
                total = (n_bits[t] + s_bits[t]) + (e_bits + w_bits)
                cnt[half, t, pl.ds(r0 - FIRST, HALO), :] = total & here[t]

    for c in force_copies:
        c.wait_recv()
    third_tile(fx.at[3], f_th[3], [f_co[i, 3] for i in range(4)])
    for i in range(n_tiles):
        rows = pl.ds(HALO + i * HALO, HALO)
        for t in range(3):
            value = zx[t, rows, :] + inv[t, rows, :] * fx[3, t, rows, :]
            zx[t, rows, :] = value
            xb[t, rows, :] = mx[t, rows, :] * value
            yb[t, rows, :] = lx[t, rows, :] * value
    for i in range(n_tiles):
        r0 = HALO + i * HALO
        rows = pl.ds(r0, HALO)
        moved = apply(xb, yb, r0)
        for t in range(3):
            value = zx[t, rows, :] + moved[t]
            ext_ref[1, t, rows, :] = value
            xa[t, rows, :] = mx[t, rows, :] * value
            ya[t, rows, :] = lx[t, rows, :] * value
    for i in range(n_tiles):
        r0 = HALO + i * HALO
        rows = pl.ds(r0, HALO)
        moved = apply(xa, ya, r0)
        for t in range(3):
            xb[t, rows, :] = moved[t]
            yb[t, rows, :] = lx[t, rows, :] * moved[t]
    for i in range(n_tiles):
        r0 = HALO + i * HALO
        rows = pl.ds(r0, HALO)
        moved = apply(xb, yb, r0)
        for t in range(3):
            ext_ref[2, t, rows, :] = moved[t]

    for c in tracer_copies:
        c.wait_recv()
    for plane in range(2 * LEVELS):
        for t in range(2):
            psc[plane, t, pl.ds(HALO - 1, 1), :] = got_w[pl.ds(2 * plane + t, 1), :]
            psc[plane, t, pl.ds(HALO + ROWS, 1), :] = got_e[pl.ds(2 * plane + t, 1), :]
    for h in range(2):
        turned_p[h, pl.ds(0, planes, stride=2), :] = jnp.where(gy < ny - 1, got_n[h], 0.0)
        turned_p[h, pl.ds(1, planes, stride=2), :] = jnp.where(gy > 0, got_s[h], 0.0)
        edge[pl.ds(h * LANES, LANES), :] = jnp.transpose(turned_p[h])
    c_u.wait()
    c_v.wait()

    def step_chunk(i, carry):
        row = pl.multiple_of(i * CHUNK, CHUNK)
        tracer_chunk(i, trs, us, vs, psc, own_ref, cnt, edge, out_ref, row)
        return carry

    lax.fori_loop(0, FIRST_CHUNKS, step_chunk, 0)

    for c in across:
        c.wait_recv()
    largest = mine[...]
    for d in range(len(across)):
        largest = jnp.maximum(largest, max_x[d])
    mid[...] = largest
    along = [remote(mid, max_y.at[d], mate) for d, mate in enumerate(line_mates)]

    lax.fori_loop(FIRST_CHUNKS, STEP_CHUNKS, step_chunk, 0)

    for c in along:
        c.wait_recv()
    for d in range(len(along)):
        largest = jnp.maximum(largest, max_y[d])
    peak_ref[...] = largest
    for c in depth_copies + field_copies + tracer_copies + force_copies + across + along:
        c.wait_send()


def finish_kernel(
    big, ext, own, peak, trs, us, vs, psc, cnt, edge,
    tr_out, surf_out, tx_out, ty_out,
    sx, stage, late, sem, late_sem, out_sem,
):
    copies = []
    done = pl.ds(0, STEP_CHUNKS * CHUNK)
    for c in range(2):
        for q in range(4):
            levels = pl.ds(4 * q, 4)
            copies.append(
                pltpu.make_async_copy(
                    big.at[c, levels], tr_out.at[c, levels, done, :], sem.at[4 * c + q]
                )
            )
    for c in copies:
        c.start()

    def late_copy(i):
        row = pl.multiple_of(i * CHUNK, CHUNK)
        left = pl.multiple_of(row - STEP_CHUNKS * CHUNK, CHUNK)
        return pltpu.make_async_copy(
            late.at[:, :, pl.ds(left, CHUNK), :],
            tr_out.at[:, :, pl.ds(row, CHUNK), :],
            late_sem.at[i - STEP_CHUNKS],
        )

    def late_chunk(i, carry):
        left = pl.multiple_of((i - STEP_CHUNKS) * CHUNK, CHUNK)
        tracer_chunk(i, trs, us, vs, psc, own, cnt, edge, late, left)
        late_copy(i).start()
        return carry

    lax.fori_loop(STEP_CHUNKS, NCHUNKS, late_chunk, 0)
    top = jnp.zeros((HALO, LANES), F32) + jnp.max(peak[...], axis=(0, 1), keepdims=True)
    lowest = 0.5 / top
    scale = 1.0 / (1.0 - lowest)
    four = 4.0 * scale * scale
    w2 = 1.0 / (1.0 - 2.0 / four)
    w3 = 1.0 / (1.0 - w2 / four)
    w4 = 1.0 / (1.0 - w3 / four)
    c0 = 1.0 - (w2 - 1.0) * (w4 - 1.0)
    c2 = w2 * w3 * w4
    for i in range((EXT - 2 * HALO) // HALO):
        rows = pl.ds(HALO + i * HALO, HALO)
        for t in range(3):
            sx[t, rows, :] = ext[0, t, rows, :] + (c0 * ext[1, t, rows, :] + c2 * ext[2, t, rows, :])
    lanes8 = lane_ids(HALO)
    for i in range(ROWS // HALO):
        r0 = FIRST + i * HALO
        rows, dst = pl.ds(r0, HALO), pl.ds(i * HALO, HALO)
        surf = [sx[t, rows, :] for t in range(3)]
        n_val, s_val = to_north(surf, lanes8), to_south(surf, lanes8)
        for t in range(2):
            lanes = pl.ds(t * LANES, LANES)
            wet = jnp.where(own[2, t, dst, :] > 0.0, 0.25, 0.0)
            diff = sx[t, pl.ds(r0 + 1, HALO), :] - sx[t, pl.ds(r0 - 1, HALO), :]
            stage[0, dst, lanes] = surf[t]
            stage[1, dst, lanes] = own[0, t, dst, :] - wet * diff
            stage[2, dst, lanes] = own[1, t, dst, :] - wet * (n_val[t] - s_val[t])
    ends = []
    for i, ref in enumerate((surf_out, tx_out, ty_out)):
        ends.append(pltpu.make_async_copy(stage.at[i], ref, out_sem.at[i]))
    for c in ends:
        c.start()
    for c in copies + ends:
        c.wait()
    for i in range(STEP_CHUNKS, NCHUNKS):
        late_copy(i).wait()


def in_hbm(value):
    return pltpu.with_memory_space_constraint(value, pltpu.HBM)


def local(tracer, zonal, merid, surface, flow_x, flow_y, land_mask, levels):
    hbm = pl.BlockSpec(memory_space=pltpu.HBM)
    vmem = pl.BlockSpec(memory_space=pltpu.VMEM)
    wide = pltpu.VMEM((3, EXT, LANES), F32)
    n_remote = 28 + 15 + 7
    planes = 2 * LEVELS
    left = ROWS - STEP_CHUNKS * CHUNK
    args = (tracer, zonal, merid, surface, flow_x, flow_y, land_mask, levels)
    kept = pl.pallas_call(
        step_kernel,
        out_shape=(
            pltpu.VMEM((2, LEVELS, STEP_CHUNKS * CHUNK, COLS), F32),
            pltpu.VMEM((3, 3, EXT, LANES), F32),
            pltpu.VMEM((3, 2, ROWS, LANES), F32),
            pltpu.VMEM((HALO, LANES), F32),
            pltpu.VMEM((2, LEVELS, ROWS, COLS), F32),
            pltpu.VMEM((LEVELS, ROWS, COLS), jnp.bfloat16),
            pltpu.VMEM((LEVELS, ROWS, COLS), jnp.bfloat16),
            pltpu.VMEM((planes, 2, ROWS + 2 * HALO, LANES), F32),
            pltpu.VMEM((2, 2, ROWS, LANES), I32),
            pltpu.VMEM((2 * LANES, LANES), F32),
        ),
        in_specs=[hbm] * 8,
        out_specs=(vmem,) * 10,
        scratch_shapes=[
            pltpu.VMEM((2, ROWS, LANES), I32),
            pltpu.VMEM((2, ROWS, LANES), I32),
            pltpu.VMEM((2, 2, ROWS, LANES), F32),
            wide,
            pltpu.VMEM((4, 3, EXT, LANES), F32),
            wide, wide, wide, wide, wide, wide, wide, wide, wide,
            pltpu.VMEM((2 * planes, LANES), F32),
            pltpu.VMEM((2 * planes, LANES), F32),
            pltpu.VMEM((2 * planes, LANES), F32),
            pltpu.VMEM((2 * planes, LANES), F32),
            pltpu.VMEM((2 * LANES, LANES), F32),
            pltpu.VMEM((2, LANES, LANES), F32),
            pltpu.VMEM((2, planes, LANES), F32),
            pltpu.VMEM((2, planes, LANES), F32),
            pltpu.VMEM((2, planes, LANES), F32),
            pltpu.VMEM((2, planes, LANES), F32),
            pltpu.VMEM((HALO, ROWS), F32),
            pltpu.VMEM((HALO, ROWS), F32),
            pltpu.VMEM((LANES, ROWS), F32),
            pltpu.VMEM((4, HALO, LANES), F32),
            pltpu.VMEM((4, HALO, ROWS), F32),
            pltpu.VMEM((4, HALO, ROWS), F32),
            pltpu.VMEM((4, LANES, ROWS), F32),
            pltpu.VMEM((4, 4, HALO, LANES), F32),
            pltpu.VMEM((HALO, LANES), F32),
            pltpu.VMEM((HALO, LANES), F32),
            pltpu.VMEM((15, HALO, LANES), F32),
            pltpu.VMEM((7, HALO, LANES), F32),
            pltpu.SemaphoreType.DMA((10,)),
            pltpu.SemaphoreType.DMA((NGROUPS,)),
            pltpu.SemaphoreType.DMA((2,)),
            pltpu.SemaphoreType.DMA((n_remote,)),
            pltpu.SemaphoreType.DMA((n_remote,)),
        ],
        compiler_params=pltpu.CompilerParams(
            collective_id=1, has_side_effects=True, vmem_limit_bytes=20 << 20
        ),
        name="ocean_step",
    )(*[in_hbm(a) for a in args])
    return pl.pallas_call(
        finish_kernel,
        out_shape=(
            jax.ShapeDtypeStruct((2, LEVELS, ROWS, COLS), F32),
            jax.ShapeDtypeStruct((ROWS, COLS), F32),
            jax.ShapeDtypeStruct((ROWS, COLS), F32),
            jax.ShapeDtypeStruct((ROWS, COLS), F32),
        ),
        in_specs=[vmem] * 10,
        out_specs=(hbm,) * 4,
        scratch_shapes=[
            wide,
            pltpu.VMEM((3, ROWS, COLS), F32),
            pltpu.VMEM((2, LEVELS, left, COLS), F32),
            pltpu.SemaphoreType.DMA((8,)),
            pltpu.SemaphoreType.DMA((left // CHUNK,)),
            pltpu.SemaphoreType.DMA((3,)),
        ],
        compiler_params=pltpu.CompilerParams(vmem_limit_bytes=20 << 20),
        name="ocean_finish",
    )(*kept)


def solution(mesh):
    flat = P("gx", "gy")
    deep = P(None, "gx", "gy")
    full = P(None, None, "gx", "gy")
    return jax.shard_map(
        local,
        mesh=mesh,
        in_specs=(full, deep, deep, flat, flat, flat, flat, flat),
        out_specs=(full, flat, flat, flat),
        check_vma=False,
    )
```

profile of v0, /device:TPU:1, one launch (start us, length us, event | category | flops | bytes accessed | tf_op | source)
XLA Modules:
  0.0 27.9 jit_solution(3064551587944473499)
XLA Ops:
  0.6 24.0 %ocean_step.1 = (f32[2,16,176,256]{3,2,1,0:T(8,128)S(1)}, f32[3,3,256,128]{3,2,1,0:T(8,128)S(1)}, f32[3,2,224,128]{3,2,1,0:T(8,128)S(1)}, f32[8,128]{1,0:T(8,128...) custom-call(f32[2,16,224,256]{3,2,1,0:T(8,128)} %tr_hbm.1, ...), custom_call_target="tpu_custom_call" | custom-call | tf_op jit(solution)/shard_map/ocean_step/pallas_call | solution.py:547
  24.6 3.3 %ocean_finish.1 = (f32[2,16,224,256]{3,2,1,0:T(8,128)}, f32[224,256]{1,0:T(8,128)}, f32[224,256]{1,0:T(8,128)}, f32[224,256]{1,0:T(8,128)}) custom-call(f32[2,16,176,256]{3,2,1,0:T(8,128)S(1)} %get-tuple-element.14.big, f32[3,3,256,128]{3,2,1,0:T(8,128)S(1)} %get-tuple-element.15.ext, f32[3,2,224,128]{3,2,1,0:T(8,128)S(1)} %get-tuple-element.16.own, ...), custom_call_target="tpu_custom_call" | custom-call | tf_op jit(solution)/shard_map/ocean_finish/pallas_call | solution.py:603
where the time goes:
time: 28 us; the launch traced here: 27.9 us
  Pallas kernels  27.2 us (97%)
  between operations  0.64 us (2%)
    pallas_call x1, Pallas kernels, local(): pl.pallas_call(step_kernel, out_shape=(pltpu.VMEM((2, LEVELS, STEP_CHUNKS...  24 us
    pallas_call x1, Pallas kernels, local(): pl.pallas_call(finish_kernel, out_shape=(jax.ShapeDtypeStruct((2, LEVELS,...  3.29 us

commit v1 on v0

--- a/solution.py
+++ b/solution.py
@@ -21,7 +21,7 @@
 NGROUPS = ROWS // GROUP
 CHUNK = 16
 NCHUNKS = ROWS // CHUNK
-EARLY_GROUPS = 2
+EARLY_GROUPS = 1
 FIRST_CHUNKS = 2
 STEP_CHUNKS = 11
 
@@ -119,10 +119,11 @@
         (lax.rem(ring + d % 4, 4) * 4 + x_hi * 2 + lax.rem(core + d // 4, 2), gy)
         for d in range(1, 8)
     ]
-    sides = ((east, gy), (west, gy), (gx, north), (gx, south))
+    sides = ((east, gy), (west, gy))
 
     barrier = pltpu.get_barrier_semaphore()
-    greeted = (*plane_mates, *line_mates, *sides, *corners)
+    plane_order = (9, 13, 8, 10, 12, 14, 7, 11, 1, 5, 0, 2, 4, 6, 3)
+    greeted = (*corners, *sides, *[plane_mates[d] for d in plane_order], *line_mates)
     for mate in greeted:
         pl.semaphore_signal(barrier, inc=1, device_id=mate, device_id_type=MESH)
 
@@ -223,8 +224,6 @@
         return carry
 
     lax.fori_loop(0, EARLY_GROUPS, force_group, 0)
-    c_u.start()
-    c_v.start()
 
     pl.semaphore_wait(barrier, len(greeted))
 
@@ -273,6 +272,8 @@
     field_copies = send_fields(pl.ds(0, 3))
 
     lax.fori_loop(EARLY_GROUPS, NGROUPS, force_group, 0)
+    c_u.start()
+    c_v.start()
     for plane in range(2 * LEVELS):
         for t in range(2):
             row_w[pl.ds(2 * plane + t, 1), :] = psc[plane, t, pl.ds(HALO, 1), :]
@@ -314,113 +315,142 @@
             if t == 2 or i == 0 or i == n_tiles - 1:
                 mx[t, rows, :] = jnp.where(lx[t, rows, :] > 0.0, 1.0, 0.0)
 
-    largest = jnp.zeros((HALO, LANES), F32)
-    for i in range(n_tiles):
-        r0 = HALO + i * HALO
-        rows = pl.ds(r0, HALO)
-        sum_m = nine_sum(mx, r0, HALO, lanes8)
-        sum_l = nine_sum(lx, r0, HALO, lanes8)
+    lanes16 = lane_ids(CHUNK)
+
+    def diagonal(r0, size, lanes):
+        rows = pl.ds(r0, size)
+        sum_m = nine_sum(mx, r0, size, lanes)
+        sum_l = nine_sum(lx, r0, size, lanes)
+        values = []
         for t in range(3):
             value = 0.5 + 0.125 * (lx[t, rows, :] * sum_m[t] + mx[t, rows, :] * sum_l[t])
             inv[t, rows, :] = value
-            if t < 2 and FIRST <= r0 < LAST:
-                largest = jnp.maximum(largest, value)
-    mine[...] = largest
-
-    across = [remote(mine, max_x.at[d], mate) for d, mate in enumerate(plane_mates)]
-
-    keep8 = inside(lanes8)
-    for i in range(n_tiles):
-        rows = pl.ds(HALO + i * HALO, HALO)
+            values.append(value)
+        return values
+
+    def diagonal_rows(i, largest):
+        values = diagonal(FIRST + i * CHUNK, CHUNK, lanes16)
+        return jnp.maximum(largest, jnp.maximum(values[0], values[1]))
+
+    largest = jnp.zeros((CHUNK, LANES), F32)
+    for i in range(NCHUNKS):
+        largest = diagonal_rows(i, largest)
+    mine[...] = jnp.maximum(largest[:HALO], largest[HALO:])
+
+    across = [remote(mine, max_x.at[d], plane_mates[d]) for d in plane_order]
+
+    def each_row(body):
+        for i in range((EXT - 2 * HALO) // CHUNK):
+            body(HALO + i * CHUNK)
+
+    diagonal(FIRST - HALO, HALO, lanes8)
+    diagonal(LAST, HALO, lanes8)
+    keep16 = inside(lanes16)
+
+    def weights(r0):
+        rows = pl.ds(r0, CHUNK)
         for t in range(3):
             recip = 1.0 / inv[t, rows, :]
             if t == 2:
-                recip = jnp.where(keep8, recip, 0.0)
+                recip = jnp.where(keep16, recip, 0.0)
             inv[t, rows, :] = recip
             eighth = 0.125 * recip
             a1[t, rows, :] = eighth * lx[t, rows, :]
             a2[t, rows, :] = eighth * mx[t, rows, :]
 
+    each_row(weights)
+
     for c in field_copies:
         c.wait_recv()
     for f in range(3):
         third_tile(fx.at[f], f_th[f], [f_co[i, f] for i in range(4)])
-    for i in range(n_tiles):
-        rows = pl.ds(HALO + i * HALO, HALO)
+
+    def split_start(r0):
+        rows = pl.ds(r0, CHUNK)
         for t in range(3):
             value = fx[0, t, rows, :]
             ext_ref[0, t, rows, :] = value
             xa[t, rows, :] = mx[t, rows, :] * value
             ya[t, rows, :] = lx[t, rows, :] * value
 
+    each_row(split_start)
+
     def apply(x_ref, y_ref, r0):
-        rows = pl.ds(r0, HALO)
-        sum_x = nine_sum(x_ref, r0, HALO, lanes8)
-        sum_y = nine_sum(y_ref, r0, HALO, lanes8)
+        rows = pl.ds(r0, CHUNK)
+        sum_x = nine_sum(x_ref, r0, CHUNK, lanes16)
+        sum_y = nine_sum(y_ref, r0, CHUNK, lanes16)
         return [a1[t, rows, :] * sum_x[t] + a2[t, rows, :] * sum_y[t] for t in range(3)]
 
-    for i in range(n_tiles):
-        r0 = HALO + i * HALO
-        rows = pl.ds(r0, HALO)
+    def first_part(r0):
+        rows = pl.ds(r0, CHUNK)
         moved = apply(xa, ya, r0)
         flux = [fx[2, t, rows, :] for t in range(3)]
-        flux_n, flux_s = to_north(flux, lanes8), to_south(flux, lanes8)
-        for t in range(3):
-            div = fx[1, t, pl.ds(r0 + 1, HALO), :] - fx[1, t, pl.ds(r0 - 1, HALO), :]
+        flux_n, flux_s = to_north(flux, lanes16), to_south(flux, lanes16)
+        for t in range(3):
+            div = fx[1, t, pl.ds(r0 + 1, CHUNK), :] - fx[1, t, pl.ds(r0 - 1, CHUNK), :]
             div = div + (flux_n[t] - flux_s[t])
             zx[t, rows, :] = (moved[t] - fx[0, t, rows, :]) - 0.25 * inv[t, rows, :] * div
+
+    each_row(first_part)
 
     def marks(depth, base):
         count = jnp.clip(depth.astype(I32) - base, 0, 8)
         return jnp.left_shift(jnp.ones_like(count), 3 * count) - 1
 
     each = 0o11111111
-    for i in range(ROWS // HALO):
-        r0 = FIRST + i * HALO
-        rows = pl.ds(r0, HALO)
+    def count_wet(i):
+        r0 = FIRST + i * CHUNK
+        rows = pl.ds(r0, CHUNK)
         for half in range(2):
             base = 8 * half
             here = [marks(lx[t, rows, :], base) for t in range(3)]
             bits = [h & each for h in here]
-            n_bits, s_bits = to_north(bits, lanes8), to_south(bits, lanes8)
+            n_bits, s_bits = to_north(bits, lanes16), to_south(bits, lanes16)
             for t in range(2):
-                e_bits = marks(lx[t, pl.ds(r0 + 1, HALO), :], base) & each
-                w_bits = marks(lx[t, pl.ds(r0 - 1, HALO), :], base) & each
+                e_bits = marks(lx[t, pl.ds(r0 + 1, CHUNK), :], base) & each
+                w_bits = marks(lx[t, pl.ds(r0 - 1, CHUNK), :], base) & each
                 total = (n_bits[t] + s_bits[t]) + (e_bits + w_bits)
-                cnt[half, t, pl.ds(r0 - FIRST, HALO), :] = total & here[t]
+                cnt[half, t, pl.ds(i * CHUNK, CHUNK), :] = total & here[t]
+
+    for i in range(NCHUNKS):
+        count_wet(i)
 
     for c in force_copies:
         c.wait_recv()
     third_tile(fx.at[3], f_th[3], [f_co[i, 3] for i in range(4)])
-    for i in range(n_tiles):
-        rows = pl.ds(HALO + i * HALO, HALO)
+
+    def add_force(r0):
+        rows = pl.ds(r0, CHUNK)
         for t in range(3):
             value = zx[t, rows, :] + inv[t, rows, :] * fx[3, t, rows, :]
             zx[t, rows, :] = value
             xb[t, rows, :] = mx[t, rows, :] * value
             yb[t, rows, :] = lx[t, rows, :] * value
-    for i in range(n_tiles):
-        r0 = HALO + i * HALO
-        rows = pl.ds(r0, HALO)
+
+    def first_power(r0):
+        rows = pl.ds(r0, CHUNK)
         moved = apply(xb, yb, r0)
         for t in range(3):
             value = zx[t, rows, :] + moved[t]
             ext_ref[1, t, rows, :] = value
             xa[t, rows, :] = mx[t, rows, :] * value
             ya[t, rows, :] = lx[t, rows, :] * value
-    for i in range(n_tiles):
-        r0 = HALO + i * HALO
-        rows = pl.ds(r0, HALO)
+
+    def second_power(r0):
+        rows = pl.ds(r0, CHUNK)
         moved = apply(xa, ya, r0)
         for t in range(3):
             xb[t, rows, :] = moved[t]
             yb[t, rows, :] = lx[t, rows, :] * moved[t]
-    for i in range(n_tiles):
-        r0 = HALO + i * HALO
-        rows = pl.ds(r0, HALO)
+
+    def third_power(r0):
+        rows = pl.ds(r0, CHUNK)
         moved = apply(xb, yb, r0)
         for t in range(3):
             ext_ref[2, t, rows, :] = moved[t]
+
+    for body in (add_force, first_power, second_power, third_power):
+        each_row(body)
 
     for c in tracer_copies:
         c.wait_recv()

time: 28 us -> 27.6 us (0.986)
  Pallas kernels: 27.2 us -> 26.8 us
    pallas_call x1, Pallas kernels: 24 us -> 23.5 us  [local(): pl.pallas_call(step_kernel, out_shape=(pltpu.VMEM((2, LEVELS, STEP_CHUNKS...]
where the time goes in v1:
time: 27.6 us; the launch traced here: 27.5 us
  Pallas kernels  26.8 us (97%)
  between operations  0.64 us (2%)
    pallas_call x1, Pallas kernels, local(): pl.pallas_call(step_kernel, out_shape=(pltpu.VMEM((2, LEVELS, STEP_CHUNKS...  23.5 us
    pallas_call x1, Pallas kernels, local(): pl.pallas_call(finish_kernel, out_shape=(jax.ShapeDtypeStruct((2, LEVELS,...  3.29 us

profile of v1, /device:TPU:1, one launch (start us, length us, event | category | flops | bytes accessed | tf_op | source)
XLA Modules:
  0.0 27.5 jit_solution(2370994307742974449)
XLA Ops:
  0.6 23.5 %ocean_step.1 = (f32[2,16,176,256]{3,2,1,0:T(8,128)S(1)}, f32[3,3,256,128]{3,2,1,0:T(8,128)S(1)}, f32[3,2,224,128]{3,2,1,0:T(8,128)S(1)}, f32[8,128]{1,0:T(8,128...) custom-call(f32[2,16,224,256]{3,2,1,0:T(8,128)} %tr_hbm.1, ...), custom_call_target="tpu_custom_call" | custom-call | tf_op jit(solution)/shard_map/ocean_step/pallas_call | solution.py:577
  24.2 3.3 %ocean_finish.1 = (f32[2,16,224,256]{3,2,1,0:T(8,128)}, f32[224,256]{1,0:T(8,128)}, f32[224,256]{1,0:T(8,128)}, f32[224,256]{1,0:T(8,128)}) custom-call(f32[2,16,176,256]{3,2,1,0:T(8,128)S(1)} %get-tuple-element.14.big, f32[3,3,256,128]{3,2,1,0:T(8,128)S(1)} %get-tuple-element.15.ext, f32[3,2,224,128]{3,2,1,0:T(8,128)S(1)} %get-tuple-element.16.own, ...), custom_call_target="tpu_custom_call" | custom-call | tf_op jit(solution)/shard_map/ocean_finish/pallas_call | solution.py:633

commit v2 on v1

--- a/solution.py
+++ b/solution.py
@@ -21,7 +21,6 @@
 NGROUPS = ROWS // GROUP
 CHUNK = 16
 NCHUNKS = ROWS // CHUNK
-EARLY_GROUPS = 1
 FIRST_CHUNKS = 2
 STEP_CHUNKS = 11
 
@@ -168,17 +167,51 @@
     for t in range(2):
         depth = (lev_s[t] * mask_s[t]).astype(F32)
         lx[t, pl.ds(FIRST, ROWS), :] = depth
-        own_ref[2, t] = depth
-        mx[t, pl.ds(FIRST, ROWS), :] = jnp.where(depth > 0.0, 1.0, 0.0)
         turned = jnp.transpose(depth)
         if t == 0:
             l_s[...] = turned[:HALO]
         else:
             l_n[...] = turned[LANES - HALO :]
+
+    pl.semaphore_wait(barrier, len(greeted))
+
+    started = [0]
+
+    def remote(src, dst, who):
+        slot = started[0]
+        started[0] += 1
+        copy = pltpu.make_async_remote_copy(
+            src_ref=src,
+            dst_ref=dst,
+            send_sem=send_sem.at[slot],
+            recv_sem=recv_sem.at[slot],
+            device_id=who,
+            device_id_type=MESH,
+        )
+        copy.start()
+        return copy
+
+    high, low = pl.ds(LAST - HALO, HALO), pl.ds(FIRST, HALO)
+    below, above = pl.ds(FIRST - HALO, HALO), pl.ds(LAST, HALO)
+    both = pl.ds(0, 2)
+    depth_copies = [
+        remote(lx.at[1, high, :], l_co.at[0], (east, north)),
+        remote(lx.at[0, high, :], l_co.at[1], (east, south)),
+        remote(lx.at[1, low, :], l_co.at[2], (west, north)),
+        remote(lx.at[0, low, :], l_co.at[3], (west, south)),
+        remote(lx.at[both, high, :], lx.at[both, below, :], (east, gy)),
+        remote(lx.at[both, low, :], lx.at[both, above, :], (west, gy)),
+        remote(l_n, l_th.at[pl.ds(LANES - HALO, HALO), :], (gx, north)),
+        remote(l_s, l_th.at[pl.ds(0, HALO), :], (gx, south)),
+    ]
+
     for c in c_tx + c_ty + c_e0:
         c.wait()
     for t in range(2):
-        wet = lx[t, pl.ds(FIRST, ROWS), :] > 0.0
+        depth = lx[t, pl.ds(FIRST, ROWS), :]
+        own_ref[2, t] = depth
+        wet = depth > 0.0
+        mx[t, pl.ds(FIRST, ROWS), :] = jnp.where(wet, 1.0, 0.0)
         for i in range(2):
             value = jnp.where(wet, raw_s[i, t], 0.0)
             own_ref[i, t] = value
@@ -190,6 +223,20 @@
 
     for f in range(3):
         turn_edges(f)
+
+    def send_fields(which):
+        return [
+            remote(fx.at[which, both, high, :], fx.at[which, both, below, :], (east, gy)),
+            remote(fx.at[which, both, low, :], fx.at[which, both, above, :], (west, gy)),
+            remote(f_n.at[which], f_th.at[which, pl.ds(LANES - HALO, HALO), :], (gx, north)),
+            remote(f_s.at[which], f_th.at[which, pl.ds(0, HALO), :], (gx, south)),
+            remote(fx.at[which, 1, high, :], f_co.at[0, which], (east, north)),
+            remote(fx.at[which, 0, high, :], f_co.at[1, which], (east, south)),
+            remote(fx.at[which, 1, low, :], f_co.at[2, which], (west, north)),
+            remote(fx.at[which, 0, low, :], f_co.at[3, which], (west, south)),
+        ]
+
+    field_copies = send_fields(pl.ds(0, 3))
 
     glanes = lane_ids(GROUP)
 
@@ -223,55 +270,7 @@
             fx[3, t, rows, :] = total[t] * (1.0 / LEVELS) + 0.5 * fx[0, t, rows, :]
         return carry
 
-    lax.fori_loop(0, EARLY_GROUPS, force_group, 0)
-
-    pl.semaphore_wait(barrier, len(greeted))
-
-    started = [0]
-
-    def remote(src, dst, who):
-        slot = started[0]
-        started[0] += 1
-        copy = pltpu.make_async_remote_copy(
-            src_ref=src,
-            dst_ref=dst,
-            send_sem=send_sem.at[slot],
-            recv_sem=recv_sem.at[slot],
-            device_id=who,
-            device_id_type=MESH,
-        )
-        copy.start()
-        return copy
-
-    high, low = pl.ds(LAST - HALO, HALO), pl.ds(FIRST, HALO)
-    below, above = pl.ds(FIRST - HALO, HALO), pl.ds(LAST, HALO)
-    both = pl.ds(0, 2)
-    depth_copies = [
-        remote(lx.at[1, high, :], l_co.at[0], (east, north)),
-        remote(lx.at[0, high, :], l_co.at[1], (east, south)),
-        remote(lx.at[1, low, :], l_co.at[2], (west, north)),
-        remote(lx.at[0, low, :], l_co.at[3], (west, south)),
-        remote(lx.at[both, high, :], lx.at[both, below, :], (east, gy)),
-        remote(lx.at[both, low, :], lx.at[both, above, :], (west, gy)),
-        remote(l_n, l_th.at[pl.ds(LANES - HALO, HALO), :], (gx, north)),
-        remote(l_s, l_th.at[pl.ds(0, HALO), :], (gx, south)),
-    ]
-
-    def send_fields(which):
-        return [
-            remote(fx.at[which, both, high, :], fx.at[which, both, below, :], (east, gy)),
-            remote(fx.at[which, both, low, :], fx.at[which, both, above, :], (west, gy)),
-            remote(f_n.at[which], f_th.at[which, pl.ds(LANES - HALO, HALO), :], (gx, north)),
-            remote(f_s.at[which], f_th.at[which, pl.ds(0, HALO), :], (gx, south)),
-            remote(fx.at[which, 1, high, :], f_co.at[0, which], (east, north)),
-            remote(fx.at[which, 0, high, :], f_co.at[1, which], (east, south)),
-            remote(fx.at[which, 1, low, :], f_co.at[2, which], (west, north)),
-            remote(fx.at[which, 0, low, :], f_co.at[3, which], (west, south)),
-        ]
-
-    field_copies = send_fields(pl.ds(0, 3))
-
-    lax.fori_loop(EARLY_GROUPS, NGROUPS, force_group, 0)
+    lax.fori_loop(0, NGROUPS, force_group, 0)
     c_u.start()
     c_v.start()
     for plane in range(2 * LEVELS):

time: 27.6 us -> 27.3 us (0.989)
  Pallas kernels: 26.8 us -> 26.5 us
    pallas_call x1, Pallas kernels: 23.5 us -> 23.2 us  [local(): pl.pallas_call(step_kernel, out_shape=(pltpu.VMEM((2, LEVELS, STEP_CHUNKS...]
where the time goes in v2:
time: 27.3 us; the launch traced here: 27.2 us
  Pallas kernels  26.5 us (97%)
  between operations  0.64 us (2%)
    pallas_call x1, Pallas kernels, local(): pl.pallas_call(step_kernel, out_shape=(pltpu.VMEM((2, LEVELS, STEP_CHUNKS...  23.2 us
    pallas_call x1, Pallas kernels, local(): pl.pallas_call(finish_kernel, out_shape=(jax.ShapeDtypeStruct((2, LEVELS,...  3.29 us

profile of v2, /device:TPU:1, one launch (start us, length us, event | category | flops | bytes accessed | tf_op | source)
XLA Modules:
  0.0 27.2 jit_solution(7672625012217764361)
XLA Ops:
  0.6 23.2 %ocean_step.1 = (f32[2,16,176,256]{3,2,1,0:T(8,128)S(1)}, f32[3,3,256,128]{3,2,1,0:T(8,128)S(1)}, f32[3,2,224,128]{3,2,1,0:T(8,128)S(1)}, f32[8,128]{1,0:T(8,128...) custom-call(f32[2,16,224,256]{3,2,1,0:T(8,128)} %tr_hbm.1, ...), custom_call_target="tpu_custom_call" | custom-call | tf_op jit(solution)/shard_map/ocean_step/pallas_call | solution.py:576
  23.9 3.3 %ocean_finish.1 = (f32[2,16,224,256]{3,2,1,0:T(8,128)}, f32[224,256]{1,0:T(8,128)}, f32[224,256]{1,0:T(8,128)}, f32[224,256]{1,0:T(8,128)}) custom-call(f32[2,16,176,256]{3,2,1,0:T(8,128)S(1)} %get-tuple-element.14.big, f32[3,3,256,128]{3,2,1,0:T(8,128)S(1)} %get-tuple-element.15.ext, f32[3,2,224,128]{3,2,1,0:T(8,128)S(1)} %get-tuple-element.16.own, ...), custom_call_target="tpu_custom_call" | custom-call | tf_op jit(solution)/shard_map/ocean_finish/pallas_call | solution.py:632
